TPU v7x, 32 devices: a whole 2x2x4 slice. The times are simulated.
32 devices in a mesh: grp: 4 (over y, x), occ: 8 (over z, core).
Axes of the slice: x: 2, y: 2, z: 4, core: 2. Of those that a mesh axis runs over, the one named last changes fastest.
Arguments:
- b_ints: bfloat16 [256, 768, 256], P(('grp', 'occ')), may hold values from -6 to 6
- osv_vecs: bfloat16 [256, 768, 128], P(('grp', 'occ')), may hold values from -0.21875 to 0.21875
- inv_denom: float32 [256, 128], P(('grp', 'occ')), may hold values from 0.5 to 4
- domains: int32 [256, 6], P('grp'), may hold values from 0 to 95, all different within a row
- dom_count: int32 [256], P('grp'), may hold values from 1 to 6
- owner_slot: int32 [96], replicated, may hold values from 0 to 95, each once
Outputs:
- gamma_tiles: bfloat16 [256, 96, 128], P('occ', 'grp')
Inputs may be any that keep to these rules, and one draw needn't show every extreme that they name: `domains`: each row names distinct tiles.
All inputs are finite; a program needn't handle non-finite values.
Results may differ from a plain program's by a relative error of at most 0.0056.
Values may be sent and summed in bfloat16 or wider, within the bound.
A program may use at most 64 MiB of HBM per device.

v0:
```python
import jax
import jax.numpy as jnp
from jax import lax
from jax.sharding import PartitionSpec as P


def local(b_ints, osv_vecs, inv_denom, domains, dom_count, owner_slot):
    own = b_ints.shape[0]
    kdom = domains.shape[1]
    tile = b_ints.shape[1] // kdom
    ntiles = owner_slot.shape[0]
    tiles_ids = jnp.arange(ntiles, dtype=jnp.int32)
    keep_all = jnp.arange(kdom, dtype=jnp.int32)[None, :] < dom_count[:, None]
    looked = jnp.sum(jnp.where(domains[:, :, None] == tiles_ids, owner_slot, 0), axis=-1)
    slot_all = jnp.where(keep_all, looked, -1)
    start = lax.axis_index("occ") * own
    keep = lax.dynamic_slice_in_dim(keep_all, start, own, 0)
    rowmask = jnp.repeat(keep, tile, axis=1).astype(jnp.bfloat16)
    masked = b_ints * rowmask[:, :, None]
    hidden = jnp.einsum("ikn,ikp->inp", osv_vecs, masked, preferred_element_type=jnp.float32)
    scaled = (hidden * inv_denom[:, :, None]).astype(jnp.bfloat16)
    amp = jnp.einsum("ikn,inp->pik", osv_vecs, scaled, preferred_element_type=jnp.float32)
    amp = (amp * rowmask[None].astype(jnp.float32)).astype(jnp.bfloat16)
    got = lax.all_to_all(amp, "occ", split_axis=0, concat_axis=1, tiled=True)
    inst = got.reshape(got.shape[0], -1, tile)
    onehot = (slot_all.reshape(-1)[None, :] == tiles_ids[:, None]).astype(jnp.bfloat16)
    partial_sum = jnp.einsum("sn,pna->psa", onehot, inst, preferred_element_type=jnp.float32)
    summed = lax.psum_scatter(partial_sum, "grp", scatter_dimension=1, tiled=True)
    return summed.astype(jnp.bfloat16)


def solution(mesh):
    return jax.shard_map(
        local,
        mesh=mesh,
        in_specs=(
            P(("grp", "occ"), None, None),
            P(("grp", "occ"), None, None),
            P(("grp", "occ"), None),
            P("grp", None),
            P("grp"),
            P(),
        ),
        out_specs=P("occ", "grp", None),
        check_vma=False,
    )
```

profile of v0, /device:TPU:0, one launch (start us, length us, event | category | flops | bytes accessed | tf_op | source)
XLA Modules:
  0.0 149.6 jit_solution(7063993562794874877)
XLA Ops:
  6.5 0.0 copy-start
  6.5 0.8 iota_compare_fusion.2
  7.3 0.1 dynamic-slice_convert_fusion
  7.4 0.1 broadcast_bitcast_fusion
  7.5 0.5 copy-done
  8.0 5.6 %fusion = bf16[256,8,768]{2,0,1:T(8,128)(2,1)} fusion(f32[8,768]{1,0:T(8,128)S(1)} %get-tuple-element.6, bf16[8,768,128]{2,1,0:T(8,128)(2,1)S(1)} %copy-done, bf16[8,768,256]{2,1,0:T(8,128)(2,1)} %param.6, bf16[8,768]{1,0:T(8,128)(2,1)S(1)} %get-tuple-element.5, f32[8,128]{1,0:T(8,128)} %param.8), kind=kOutput, calls=%fused_computation.1 | convolution fusion | flops 810549248 | bytes 7905280 | tf_op jit(solution)/shard_map/ikn,inp->pik/dot_general | solution.py:22
  13.6 5.3 %copy.18 = bf16[256,8,768]{2,1,0:T(8,128)(2,1)} copy(bf16[256,8,768]{2,0,1:T(8,128)(2,1)} %fusion) | data formatting | bytes 6291456 | tf_op jit(solution)/shard_map/convert_element_type | solution.py:23
  18.9 0.0 copy-start.1
  18.9 0.0 copy-start.2
  18.9 6.5 %all-to-all-start = ((bf16[256,8,768]{2,1,0:T(8,128)(2,1)}), bf16[256,8,768]{2,1,0:T(8,128)(2,1)}, u32[]{:S(2)}, u32[]{:S(2)}) async-start(bf16[256,8,768]{2,1,0:T(8,128)(2,1)} %copy.18), calls=%async_computation | async-start | bytes 6291456 | tf_op jit(solution)/shard_map/all_to_all | solution.py:24
  25.4 0.0 reduce-scatter.2.cloned.1.call-start
  25.4 0.0 copy-done.1
  25.4 0.0 copy-done.2
  25.4 0.3 select_reduce_fusion
  25.7 0.0 copy-done.3
  25.7 0.1 copy.20
  25.8 0.1 select_n.21
  26.0 71.0 %all-to-all-done = bf16[256,8,768]{2,1,0:T(8,128)(2,1)} async-done(((bf16[256,8,768]{2,1,0:T(8,128)(2,1)}), bf16[256,8,768]{2,1,0:T(8,128)(2,1)}, u32[]{:S(2)}, u32[]{:S(2)}) %all-to-all-start) | async-done | bytes 3145760 | tf_op jit(solution)/shard_map/all_to_all | solution.py:24
  97.0 4.0 %copy.23 = bf16[8,32,8,768]{3,2,0,1:T(8,128)(2,1)} copy(bf16[8,32,8,768]{3,2,1,0:T(8,128)(2,1)} %bitcast.2) | data formatting | bytes 6291456 | tf_op jit(solution)/shard_map/all_to_all | solution.py:24
  101.0 6.4 %reshape.42 = bf16[32,384,128]{2,1,0:T(8,128)(2,1)} reshape(bf16[32,8,8,768]{3,2,1,0:T(8,128)(2,1)} %bitcast.19) | data formatting | bytes 6291456 | tf_op jit(solution)/shard_map/reshape | solution.py:25
  107.3 3.7 %convolution_bitcast_fusion = f32[32,96,128]{2,1,0:T(8,128)} fusion(bf16[32,384,128]{2,1,0:T(8,128)(2,1)} %reshape.42, s32[384]{0:T(512)S(1)} %select_n.21), kind=kOutput, calls=%fused_computation.6 | convolution fusion | flops 302026752 | bytes 4720128 | tf_op jit(solution)/shard_map/sn,pna->psa/dot_general | solution.py:27
  111.0 0.0 reduce-scatter.2.cloned.1.call-update
  111.1 30.0 %reduce-scatter.2.cloned.1.call-done = f32[32,24,128]{2,1,0:T(8,128)} async-done(((f32[32,96,128]{2,1,0:T(8,128)}), f32[32,24,128]{2,1,0:T(8,128)}) %reduce-scatter.2.cloned.1.call-update) | async-done | bytes 393232 | tf_op jit(solution)/shard_map/reduce_scatter | solution.py:28
  141.1 1.7 %convert_element_type.43 = bf16[32,24,128]{2,1,0:T(8,128)(2,1)} convert(f32[32,24,128]{2,1,0:T(8,128)} %reduce-scatter.2.cloned.1.call-done) | non-fusion elementwise | flops 98304 | bytes 589824 | tf_op jit(solution)/shard_map/convert_element_type | solution.py:29
  (2 shorter events, 0.0 us)
Async XLA Ops:
  6.5 1.4 copy-start
  18.9 6.5 %copy-start.1 = (s32[64,6]{0,1:T(8,128)S(1)}, s32[64,6]{0,1:T(8,128)}, u32[]{:S(2)}) copy-start(s32[64,6]{0,1:T(8,128)} %param.9) | copy-start | bytes 4612
  18.9 6.5 %copy-start.2 = (s32[96]{0:T(128)S(1)}, s32[96]{0:T(128)}, u32[]{:S(2)}) copy-start(s32[96]{0:T(128)} %param.11) | copy-start | bytes 1156
  18.9 6.8 %copy-start.3 = (s32[64]{0:T(128)S(1)}, s32[64]{0:T(128)}, u32[]{:S(2)}) copy-start(s32[64]{0:T(128)} %param.10) | copy-start | bytes 772
  18.9 78.1 %all-to-all-start = ((bf16[256,8,768]{2,1,0:T(8,128)(2,1)}), bf16[256,8,768]{2,1,0:T(8,128)(2,1)}, u32[]{:S(2)}, u32[]{:S(2)}) async-start(bf16[256,8,768]{2,1,0:T(8,128)(2,1)} %copy.18), calls=%async_computation | async-start | bytes 6291456 | tf_op jit(solution)/shard_map/all_to_all | solution.py:24
  25.4 115.7 %reduce-scatter.2.cloned.1.call-start = ((), (), s32[]{:S(2)}) async-start(), calls=%async_computation.2 | async-start | bytes 1966080 | tf_op jit(solution)/shard_map/reduce_scatter | solution.py:28
Sparse Core Ops, SparseCore 0:
  111.2 29.8 reduce-scatter.1
where the time goes:
time: 150 us
  waiting for transfers between devices  101 us (67%)
  local copies, waits for them, and re-layouts  16.4 us (11%)
  between operations  13.4 us (9%)
  matrix products  9.35 us (6%)
  starting transfers between devices  6.49 us (4%)
  other arithmetic  2.91 us (2%)
    all_to_all x1, waiting for transfers between devices, local(): got = lax.all_to_all(amp, 'occ', split_axis=0, concat_axis=1, tiled=True)  71 us
    reduce_scatter x1, waiting for transfers between devices, local(): lax.psum_scatter(partial_sum, 'grp', scatter_dimension=1, tiled=True)  30 us
    all_to_all x1, starting transfers between devices, local(): got = lax.all_to_all(amp, 'occ', split_axis=0, concat_axis=1, tiled=True)  6.46 us
    reshape x1, local copies, waits for them, and re-layouts, local(): inst = got.reshape(got.shape[0], -1, tile)  6.37 us
    dot_general x1, matrix products, local(): jnp.einsum('ikn,inp->pik', osv_vecs, scaled, preferred_element_type=jnp.f...  5.64 us
    convert_element_type x1, local copies, waits for them, and re-layouts, local(): amp = (amp * rowmask[None].astype(jnp.float32)).astype(jnp.bfloat16)  5.3 us
    all_to_all x1, local copies, waits for them, and re-layouts, local(): got = lax.all_to_all(amp, 'occ', split_axis=0, concat_axis=1, tiled=True)  3.95 us
    dot_general x1, matrix products, local(): jnp.einsum('sn,pna->psa', onehot, inst, preferred_element_type=jnp.float32)  3.71 us
  transfers between devices with their start and end apart: 2, of which 2 were waited for; matrix products, arithmetic and copies ran while one was open for 0% of the time, Pallas kernels for 0%

commit v1 on v0

v1 whole, which is shorter than its diff:
```python
import functools

import jax
import jax.numpy as jnp
from jax import lax
from jax.experimental import pallas as pl
from jax.experimental.pallas import tpu as pltpu
from jax.sharding import PartitionSpec as P

MESH = pl.DeviceIdType.MESH
F32 = jnp.float32
BF16 = jnp.bfloat16
NX, NY, NZ, NC = 2, 2, 4, 2


def general(b_ints, osv_vecs, inv_denom, domains, dom_count, owner_slot):
    own = b_ints.shape[0]
    kdom = domains.shape[1]
    tile = b_ints.shape[1] // kdom
    ntiles = owner_slot.shape[0]
    tiles_ids = jnp.arange(ntiles, dtype=jnp.int32)
    keep_all = jnp.arange(kdom, dtype=jnp.int32)[None, :] < dom_count[:, None]
    looked = jnp.sum(jnp.where(domains[:, :, None] == tiles_ids, owner_slot, 0), axis=-1)
    slot_all = jnp.where(keep_all, looked, -1)
    start = lax.axis_index("occ") * own
    keep = lax.dynamic_slice_in_dim(keep_all, start, own, 0)
    rowmask = jnp.repeat(keep, tile, axis=1).astype(BF16)
    masked = b_ints * rowmask[:, :, None]
    hidden = jnp.einsum("ikn,ikp->inp", osv_vecs, masked, preferred_element_type=F32)
    scaled = (hidden * inv_denom[:, :, None]).astype(BF16)
    amp = jnp.einsum("ikn,inp->pik", osv_vecs, scaled, preferred_element_type=F32)
    amp = (amp * rowmask[None].astype(F32)).astype(BF16)
    got = lax.all_to_all(amp, "occ", split_axis=0, concat_axis=1, tiled=True)
    inst = got.reshape(got.shape[0], -1, tile)
    onehot = (slot_all.reshape(-1)[None, :] == tiles_ids[:, None]).astype(BF16)
    partial_sum = jnp.einsum("sn,pna->psa", onehot, inst, preferred_element_type=F32)
    summed = lax.psum_scatter(partial_sum, "grp", scatter_dimension=1, tiled=True)
    return summed.astype(BF16)


def tiles_kernel(kdom, dom_ref, cnt_ref, slot_ref, b_ref, q_ref, d_ref, out_ref, acc, stage, sems):
    i = pl.program_id(0)
    own = pl.num_programs(0)
    blocks, _, cols, tile = acc.shape
    row = lax.axis_index("occ") * own + i

    @pl.when(i == 0)
    def _():
        acc[...] = jnp.zeros_like(acc)

    q = q_ref[0]
    used = cnt_ref[row] * tile
    rows = lax.broadcasted_iota(jnp.int32, q.shape, 0)
    q = jnp.where(rows < used, q, jnp.zeros_like(q))
    hidden = lax.dot_general(b_ref[0], q, (((0,), (0,)), ((), ())), preferred_element_type=F32)
    scaled = (hidden * d_ref[pl.ds(i, 1), :]).astype(BF16)
    y = lax.dot_general(scaled, q, (((1,), (1,)), ((), ())), preferred_element_type=F32)
    for k in range(kdom):
        part = y[:, k * tile : (k + 1) * tile].astype(BF16).astype(F32)
        s = slot_ref[dom_ref[row, k]]
        acc[:, s] += part.reshape(blocks, cols, tile)

    @pl.when(i == own - 1)
    def _():
        copies = []
        for j in range(blocks):
            stage[j] = acc[j].astype(BF16)
            copies.append(pltpu.make_async_copy(stage.at[j], out_ref.at[j], sems.at[j]))
            copies[-1].start()
        for copy in copies:
            copy.wait()


def reduce_kernel(g_ref, out_ref, own, rc, sa, sb, ra, rb, sa2, sb2, ra2, rb2, sz, zin, fs,
                  l_sem, cs, cr, as_, ar, bs, br, as2, ar2, bs2, br2, zs, zr):
    g = lax.axis_index("grp")
    o = lax.axis_index("occ")
    x, y = g % NX, g // NX
    core, z = o % NC, o // NC
    half = own.shape[-2] // 2
    lo, hi = pl.ds(0, half), pl.ds(half, half)
    to_core = {"grp": g, "occ": z * NC + 1 - core}
    to_x = {"grp": y * NX + 1 - x, "occ": o}
    to_y = {"grp": (1 - y) * NX + x, "occ": o}
    dest = [3 - 3 * (z // 2), (2 + 3 * z) % 5, 1 + z % 2, z]
    down = [z // 2, z % 2, z // 2]
    middle = z % 3

    barrier = pltpu.get_barrier_semaphore()
    for dev in (to_core, to_x, to_y):
        pl.semaphore_signal(barrier, inc=1, device_id=dev, device_id_type=MESH)

    @pl.when(z > 0)
    def _():
        pl.semaphore_signal(barrier, inc=1, device_id={"grp": g, "occ": o - NC}, device_id_type=MESH)

    @pl.when(z < NZ - 1)
    def _():
        pl.semaphore_signal(barrier, inc=1, device_id={"grp": g, "occ": o + NC}, device_id_type=MESH)

    loads = [pltpu.make_async_copy(g_ref.at[dest[t] * NC + core], own.at[t], l_sem.at[t]) for t in range(NZ)]
    for t in range(NZ):
        loads[t].start()
    pl.semaphore_wait(barrier, 4 + (middle + 1) // 2)

    def remote(src, dst, send, recv, dev):
        return pltpu.make_async_remote_copy(
            src_ref=src, dst_ref=dst, send_sem=send, recv_sem=recv, device_id=dev, device_id_type=MESH)

    c0 = [remote(g_ref.at[dest[t] * NC + 1 - core], rc.at[t], cs.at[t], cr.at[t], to_core) for t in range(NZ)]
    a1 = [remote(sa.at[t], ra.at[t], as_.at[t], ar.at[t], to_x) for t in range(NZ)]
    b1 = [remote(sb.at[t], rb.at[t], bs.at[t], br.at[t], to_y) for t in range(NZ)]
    a2 = [remote(sa2.at[t], ra2.at[t], as2.at[t], ar2.at[t], to_y) for t in range(NZ)]
    b2 = [remote(sb2.at[t], rb2.at[t], bs2.at[t], br2.at[t], to_x) for t in range(NZ)]
    zc = []
    for t in range(NZ - 1):
        to_z = {"grp": g, "occ": (z + 1 - 2 * down[t]) * NC + core}
        zc.append(remote(sz.at[t], zin.at[down[t], dest[t]], zs.at[t], zr.at[down[t], dest[t]], to_z))

    for t in range(NZ):
        c0[t].start()

    def both(t, iy, ix, rows):
        return own[t, iy, ix, :, rows, :].astype(F32) + rc[t, iy, ix, :, rows, :].astype(F32)

    def first(t):
        loads[t].wait()
        c0[t].wait_recv()
        for j in range(NY):
            sa[t, j] = both(t, j, 1 - x, lo).astype(BF16)
        a1[t].start()
        for j in range(NX):
            sb[t, j] = both(t, 1 - y, j, hi).astype(BF16)
        b1[t].start()

    def second(t):
        a1[t].wait_recv()
        sa2[t] = (both(t, 1 - y, x, lo) + ra[t, 1 - y].astype(F32)).astype(BF16)
        a2[t].start()
        b1[t].wait_recv()
        sb2[t] = (both(t, y, 1 - x, hi) + rb[t, 1 - x].astype(F32)).astype(BF16)
        b2[t].start()

    def plane(t):
        a2[t].wait_recv()
        fs[:, lo, :] = both(t, y, x, lo) + ra[t, y].astype(F32) + ra2[t].astype(F32)
        b2[t].wait_recv()
        fs[:, hi, :] = both(t, y, x, hi) + rb[t, x].astype(F32) + rb2[t].astype(F32)

    def edge(t):
        @pl.when(middle == 0)
        def _():
            plane(t)
            sz[t] = fs[...].astype(BF16)
            zc[t].start()

    def inner(t):
        @pl.when(middle != 0)
        def _():
            plane(t)
            zc[t].wait_recv()
            sz[t] = (fs[...] + zin[down[t], dest[t]].astype(F32)).astype(BF16)
            zc[t].start()

    first(0)
    first(1)
    second(0)
    first(2)
    second(1)
    edge(0)
    first(3)
    second(2)
    inner(0)
    edge(1)
    second(3)
    inner(1)
    edge(2)
    inner(2)
    plane(3)

    def landed(way):
        dev = {"grp": g, "occ": z * NC + 1 - core}
        remote(sz.at[0], zin.at[way, z], zs.at[0], zr.at[way, z], dev).wait_recv()
        fs[...] += zin[way, z].astype(F32)

    @pl.when(z > 0)
    def _():
        landed(0)

    @pl.when(z < NZ - 1)
    def _():
        landed(1)

    out_ref[...] = fs[...].astype(BF16)
    for t in range(NZ):
        for copy in (c0[t], a1[t], b1[t], a2[t], b2[t]):
            copy.wait_send()
    for t in range(NZ - 1):
        zc[t].wait_send()


def staged(b_ints, osv_vecs, inv_denom, domains, dom_count, owner_slot):
    own, rows, naux = b_ints.shape
    nosv = osv_vecs.shape[2]
    kdom = domains.shape[1]
    tile = rows // kdom
    ntiles = owner_slot.shape[0]
    blocks = NZ * NC
    cols = naux // blocks
    slots = ntiles // (NX * NY)
    partial_tiles = pl.pallas_call(
        functools.partial(tiles_kernel, kdom),
        out_shape=jax.ShapeDtypeStruct((blocks, ntiles, cols, tile), BF16),
        grid_spec=pltpu.PrefetchScalarGridSpec(
            num_scalar_prefetch=3,
            grid=(own,),
            in_specs=[
                pl.BlockSpec((1, rows, naux), lambda i, *_: (i, 0, 0)),
                pl.BlockSpec((1, rows, nosv), lambda i, *_: (i, 0, 0)),
                pl.BlockSpec((own, nosv), lambda i, *_: (0, 0)),
            ],
            out_specs=pl.BlockSpec(memory_space=pl.ANY),
            scratch_shapes=[
                pltpu.VMEM((blocks, ntiles, cols, tile), F32),
                pltpu.VMEM((blocks, ntiles, cols, tile), BF16),
                pltpu.SemaphoreType.DMA((blocks,)),
            ],
        ),
        compiler_params=pltpu.CompilerParams(vmem_limit_bytes=40 << 20),
        cost_estimate=pl.CostEstimate(
            flops=4 * own * rows * naux * nosv, bytes_accessed=11 << 20, transcendentals=0),
    )(domains, dom_count, owner_slot, b_ints, osv_vecs, inv_denom)
    partial_tiles = partial_tiles.reshape(blocks, NY, NX, slots, cols, tile)
    half = cols // 2
    vm = lambda *shape: pltpu.VMEM(shape, BF16)
    dma = lambda *shape: pltpu.SemaphoreType.DMA(shape)
    summed = pl.pallas_call(
        reduce_kernel,
        out_shape=jax.ShapeDtypeStruct((slots, cols, tile), BF16),
        in_specs=[pl.BlockSpec(memory_space=pl.ANY)],
        out_specs=pl.BlockSpec(memory_space=pltpu.VMEM),
        scratch_shapes=[
            vm(NZ, NY, NX, slots, cols, tile), vm(NZ, NY, NX, slots, cols, tile),
            vm(NZ, NY, slots, half, tile), vm(NZ, NX, slots, half, tile),
            vm(NZ, NY, slots, half, tile), vm(NZ, NX, slots, half, tile),
            vm(NZ, slots, half, tile), vm(NZ, slots, half, tile),
            vm(NZ, slots, half, tile), vm(NZ, slots, half, tile),
            vm(NZ - 1, slots, cols, tile), vm(2, NZ, slots, cols, tile),
            pltpu.VMEM((slots, cols, tile), F32),
        ] + [dma(NZ)] * 11 + [dma(NZ - 1), dma(2, NZ)],
        compiler_params=pltpu.CompilerParams(
            collective_id=0, has_side_effects=True, vmem_limit_bytes=40 << 20),
        cost_estimate=pl.CostEstimate(flops=4 << 20, bytes_accessed=7 << 20, transcendentals=0),
    )(partial_tiles)
    return jnp.swapaxes(summed, 0, 1)


def solution(mesh):
    fits = mesh.shape["grp"] == NX * NY and mesh.shape["occ"] == NZ * NC
    return jax.shard_map(
        staged if fits else general,
        mesh=mesh,
        in_specs=(
            P(("grp", "occ"), None, None),
            P(("grp", "occ"), None, None),
            P(("grp", "occ"), None),
            P("grp", None),
            P("grp"),
            P(),
        ),
        out_specs=P("occ", "grp", None),
        check_vma=False,
    )
```

time: 150 us -> 53.2 us (0.35)
  waiting for transfers between devices: 101 us -> 0 us
  Pallas kernels: 0 us -> 46.1 us
  between operations: 13.4 us -> 0.02 us
  local copies, waits for them, and re-layouts: 16.4 us -> 6.82 us
  matrix products: 9.35 us -> 0 us
  starting transfers between devices: 6.49 us -> 0 us
  other arithmetic: 2.91 us -> 0 us
    all_to_all x1 -> x0, waiting for transfers between devices: 71 us -> none  [local(): got = lax.all_to_all(amp, 'occ', split_axis=0, concat_axis=1, tiled=True)]
    pallas_call x0 -> x2, Pallas kernels: none -> 46.1 us  [the longest x1 38.7 us: staged(): pl.pallas_call(reduce_kernel, out_shape=jax.ShapeDtypeStruct((slots, cols...]
    reduce_scatter x1 -> x0, waiting for transfers between devices: 30 us -> none  [local(): lax.psum_scatter(partial_sum, 'grp', scatter_dimension=1, tiled=True)]
    dot_general x2 -> x0, matrix products: 9.35 us -> none  [the longest x1 5.64 us: local(): jnp.einsum('ikn,inp->pik', osv_vecs, scaled, preferred_element_type=jnp.f...]
    all_to_all x1 -> x0, starting transfers between devices: 6.46 us -> none  [local(): got = lax.all_to_all(amp, 'occ', split_axis=0, concat_axis=1, tiled=True)]
    reshape x1 -> x0, local copies, waits for them, and re-layouts: 6.37 us -> none  [local(): inst = got.reshape(got.shape[0], -1, tile)]
    unnamed x8 -> x11, local copies, waits for them, and re-layouts: 0.5 us -> 6.07 us
    convert_element_type x1 -> x0, local copies, waits for them, and re-layouts: 5.3 us -> none  [local(): amp = (amp * rowmask[None].astype(jnp.float32)).astype(jnp.bfloat16)]
  transfers between devices with their start and end apart: 2 -> 0, of which waited for: 2 -> 0; matrix products, arithmetic and copies ran while one was open for 0% -> 0% of each run, Pallas kernels for 0% -> 0%
where the time goes in v1:
time: 53.2 us; the launch traced here: 53 us
  Pallas kernels  46.1 us (87%)
  local copies, waits for them, and re-layouts  6.82 us (13%)
    pallas_call x1, Pallas kernels, staged(): pl.pallas_call(reduce_kernel, out_shape=jax.ShapeDtypeStruct((slots, cols...  38.7 us
    pallas_call x1, Pallas kernels, staged(): pl.pallas_call(functools.partial(tiles_kernel, kdom), out_shape=jax.Shape...  7.49 us
    unnamed x11, local copies, waits for them, and re-layouts  6.07 us

profile of v1, /device:TPU:0, one launch (start us, length us, event | category | flops | bytes accessed | tf_op | source)
XLA Modules:
  0.0 53.0 jit_solution(662034774990379609)
XLA Ops:
  0.0 0.8 %copy.7.dom_ref = s32[64,6]{1,0:T(8,128)S(1)} copy(s32[64,6]{0,1:T(8,128)} %param.9) | data formatting | bytes 3072 | tf_op args[3]
  0.8 0.0 copy-start
  0.8 1.9 %copy-done = bf16[8,768,256]{2,1,0:T(8,128)(2,1)S(1)} copy-done((bf16[8,768,256]{2,1,0:T(8,128)(2,1)S(1)}, bf16[8,768,256]{2,1,0:T(8,128)(2,1)}, u32[]{:S(2)}) %copy-start) | copy-done | bytes 3145752
  2.7 0.0 copy-start.1
  2.7 1.4 %copy-done.1 = bf16[8,768,128]{2,1,0:T(8,128)(2,1)S(1)} copy-done((bf16[8,768,128]{2,1,0:T(8,128)(2,1)S(1)}, bf16[8,768,128]{2,1,0:T(8,128)(2,1)}, u32[]{:S(2)}) %copy-start.1) | copy-done | bytes 1572888
  4.1 0.0 copy-start.2
  4.1 0.7 %copy-done.2 = f32[8,128]{1,0:T(8,128)S(1)} copy-done((f32[8,128]{1,0:T(8,128)S(1)}, f32[8,128]{1,0:T(8,128)}, u32[]{:S(2)}) %copy-start.2) | copy-done | bytes 4120
  4.8 0.0 copy-start.3
  4.8 0.7 %copy-done.3 = s32[64]{0:T(128)S(1)} copy-done((s32[64]{0:T(128)S(1)}, s32[64]{0:T(128)}, u32[]{:S(2)}) %copy-start.3) | copy-done | bytes 280
  5.4 0.0 copy-start.4
  5.4 0.7 %copy-done.4 = s32[96]{0:T(128)S(1)} copy-done((s32[96]{0:T(128)S(1)}, s32[96]{0:T(128)}, u32[]{:S(2)}) %copy-start.4) | copy-done | bytes 408
  6.1 7.5 %shard_map.64 = bf16[8,96,32,128]{3,2,1,0:T(8,128)(2,1)S(1)} custom-call(s32[64,6]{1,0:T(8,128)S(1)} %copy.7.dom_ref, s32[64]{0:T(128)S(1)} %copy-done.3, s32[96]{0:T(128)S(1)} %copy-done.4, bf16[8,768,256]{2,1,0:T(8,128)(2,1)S(1)} %copy-done, bf16[8,768,128]{2,1,0:T(8,128)(2,1)S(1)} %copy-done.1, f32[8,128]{1,0:T(8,128)S(1)} %copy-done.2), custom_call_target="tpu_custom_call" | custom-call | flops 805306368 | bytes 11534336 | tf_op jit(solution)/shard_map/pallas_call | solution.py:211
  13.6 38.7 %shard_map.65 = bf16[24,32,128]{2,1,0:T(8,128)(2,1)S(1)} custom-call(bf16[8,2,2,24,32,128]{5,4,3,2,1,0:T(8,128)(2,1)S(1)} %bitcast.2), custom_call_target="tpu_custom_call" | custom-call | flops 4194304 | bytes 7340032 | tf_op jit(solution)/shard_map/pallas_call | solution.py:237
  52.2 0.8 %copy.8 = bf16[32,24,128]{2,1,0:T(8,128)(2,1)} copy(bf16[32,24,128]{2,0,1:T(8,128)(2,1)S(1)} %bitcast.3) | data formatting | bytes 393216 | tf_op jit(solution)/shard_map/transpose | solution.py:255
Async XLA Ops:
  0.8 1.9 %copy-start = (bf16[8,768,256]{2,1,0:T(8,128)(2,1)S(1)}, bf16[8,768,256]{2,1,0:T(8,128)(2,1)}, u32[]{:S(2)}) copy-start(bf16[8,768,256]{2,1,0:T(8,128)(2,1)} %b_ref.1) | copy-start | bytes 9437188
  2.7 1.4 %copy-start.1 = (bf16[8,768,128]{2,1,0:T(8,128)(2,1)S(1)}, bf16[8,768,128]{2,1,0:T(8,128)(2,1)}, u32[]{:S(2)}) copy-start(bf16[8,768,128]{2,1,0:T(8,128)(2,1)} %q_ref.1) | copy-start | bytes 4718596
  4.1 0.7 %copy-start.2 = (f32[8,128]{1,0:T(8,128)S(1)}, f32[8,128]{1,0:T(8,128)}, u32[]{:S(2)}) copy-start(f32[8,128]{1,0:T(8,128)} %d_ref.1) | copy-start | bytes 12292
  4.8 0.7 %copy-start.3 = (s32[64]{0:T(128)S(1)}, s32[64]{0:T(128)}, u32[]{:S(2)}) copy-start(s32[64]{0:T(128)} %cnt_ref.1) | copy-start | bytes 772
  5.4 0.7 %copy-start.4 = (s32[96]{0:T(128)S(1)}, s32[96]{0:T(128)}, u32[]{:S(2)}) copy-start(s32[96]{0:T(128)} %slot_ref.1) | copy-start | bytes 1156
